TPU v7x, 32 devices: a whole 2x2x4 slice. The times are simulated.
32 devices in a mesh: dp: 8 (over z, x), tensor: 4 (over y, core).
Axes of the slice: x: 2, y: 2, z: 4, core: 2. Of those that a mesh axis runs over, the one named last changes fastest.
Arguments:
- normed_hidden_state: bfloat16 [4, 512, 8192], P(None, 'dp', 'tensor'), may hold values from -6 to 6
- query_projection_weight: bfloat16 [8192, 4096], P(None, 'tensor'), may hold values from -0.0625 to 0.0625
- adapter_down_maps: bfloat16 [1024, 8192], P('dp', 'tensor'), may hold values from -0.0625 to 0.0625
- adapter_up_maps: bfloat16 [1024, 4096], P('dp', 'tensor'), may hold values from -0.75 to 0.75
- key_value_cache: bfloat16 [2, 512, 128, 512], P(None, 'dp', None, 'tensor'), may hold values from -82 to 82
- step_key_value: bfloat16 [4, 2, 512, 512], P(None, None, 'dp', 'tensor'), may hold values from -6 to 6
- cache_valid_length: int32 [512], P('dp'), may hold values from 1 to 128, as said below
- adapter_per_request: int32 [512], P('dp'), may hold values from 0 to 15, as said below
- adapter_pool_position: int32 [16], replicated, may hold values from 0 to 15, as said below
Outputs:
- attended: bfloat16 [4, 512, 4096], P(None, 'dp', 'tensor')
Inputs may be any that keep to these rules, and one draw needn't show every extreme that they name: `adapter_pool_position`: A permutation: every adapter has its own pool position, and position p is held by dp index p // 2. `adapter_per_request`: within each group of 64 consecutive requests, requests whose adapters sit on the same dp index use the same adapter; some dp index serves an adapter to every group. `cache_valid_length`: each group of 64 consecutive requests holds a request with all 128 positions valid.
All inputs are finite; a program needn't handle non-finite values.
Results may differ from a plain program's by a relative error of at most 0.015.
Values may be sent and summed in bfloat16 or wider, within the bound.
A program may use at most 192 MiB of HBM per device.

v0:
```python
import math

import jax
import jax.numpy as jnp
from jax import lax
from jax.sharding import PartitionSpec as P

HEAD_SIZE = 128
ADAPTER_RANK = 64


def pool_lookup(adapters, adapter_pool_position):
    table = jnp.arange(adapter_pool_position.shape[0], dtype=jnp.int32)
    match = adapters[:, None] == table[None, :]
    return jnp.sum(jnp.where(match, adapter_pool_position[None, :], 0), axis=1)


def adapt_rows(normed_hidden_state, down_map_pages, up_map_pages):
    shrink_local = jnp.einsum(
        "trd,rjd->trj", normed_hidden_state, down_map_pages, preferred_element_type=jnp.float32
    )
    shrink = lax.psum(shrink_local, "tensor").astype(jnp.bfloat16)
    return jnp.einsum("trj,rjh->trh", shrink, up_map_pages, preferred_element_type=jnp.float32)


def attend(query, key_value_cache, step_key_value, cache_valid_length):
    steps = step_key_value.shape[0]
    requests = step_key_value.shape[2]
    length = key_value_cache.shape[2]
    kv_local = key_value_cache.shape[3] // HEAD_SIZE
    group = query.shape[2] // HEAD_SIZE // kv_local
    scale = 1.0 / math.sqrt(HEAD_SIZE)
    grouped = query.reshape(steps, requests, kv_local, group, HEAD_SIZE)
    keys = key_value_cache[0].reshape(requests, length, kv_local, HEAD_SIZE)
    values = key_value_cache[1].reshape(requests, length, kv_local, HEAD_SIZE)
    new_keys = step_key_value[:, 0].reshape(steps, requests, kv_local, HEAD_SIZE)
    new_values = step_key_value[:, 1].reshape(steps, requests, kv_local, HEAD_SIZE)
    cache_scores = (
        jnp.einsum("trkgd,rckd->trkgc", grouped, keys, preferred_element_type=jnp.float32) * scale
    )
    valid = jnp.arange(length, dtype=jnp.int32)[None, :] < cache_valid_length[:, None]
    cache_scores = jnp.where(valid[None, :, None, None, :], cache_scores, -1e30)
    fresh_scores = (
        jnp.einsum("trkgd,srkd->trkgs", grouped, new_keys, preferred_element_type=jnp.float32)
        * scale
    )
    causal = (
        jnp.arange(steps, dtype=jnp.int32)[:, None] >= jnp.arange(steps, dtype=jnp.int32)[None, :]
    )
    fresh_scores = jnp.where(causal[:, None, None, None, :], fresh_scores, -1e30)
    top = jnp.maximum(jnp.max(cache_scores, axis=-1), jnp.max(fresh_scores, axis=-1))
    cache_expo = jnp.exp(cache_scores - top[..., None])
    fresh_expo = jnp.exp(fresh_scores - top[..., None])
    total = jnp.sum(cache_expo, axis=-1) + jnp.sum(fresh_expo, axis=-1)
    mixed = jnp.einsum(
        "trkgc,rckd->trkgd",
        cache_expo.astype(jnp.bfloat16),
        values,
        preferred_element_type=jnp.float32,
    )
    mixed = mixed + jnp.einsum(
        "trkgs,srkd->trkgd",
        fresh_expo.astype(jnp.bfloat16),
        new_values,
        preferred_element_type=jnp.float32,
    )
    attended = mixed / total[..., None]
    return attended.reshape(steps, requests, -1).astype(jnp.bfloat16)


def per_device(
    normed_hidden_state,
    query_projection_weight,
    adapter_down_maps,
    adapter_up_maps,
    key_value_cache,
    step_key_value,
    cache_valid_length,
    adapter_per_request,
    adapter_pool_position,
):
    steps, requests, part_width = normed_hidden_state.shape
    count_rows = steps * requests
    token_rows = normed_hidden_state.reshape(count_rows, part_width)
    heads_width = query_projection_weight.shape[1]
    position = pool_lookup(adapter_per_request, adapter_pool_position)
    base = jnp.dot(
        lax.all_gather(token_rows, "tensor", axis=1, tiled=True),
        query_projection_weight,
        preferred_element_type=jnp.float32,
    )
    down_all, up_all = (
        lax.all_gather(adapter_down_maps, "dp", axis=0, tiled=True),
        lax.all_gather(adapter_up_maps, "dp", axis=0, tiled=True),
    )
    down_map_pages = jnp.take(down_all.reshape(-1, ADAPTER_RANK, part_width), position, axis=0)
    up_map_pages = jnp.take(up_all.reshape(-1, ADAPTER_RANK, heads_width), position, axis=0)
    delta = adapt_rows(normed_hidden_state, down_map_pages, up_map_pages)
    query = (base.reshape(steps, requests, heads_width) + delta).astype(jnp.bfloat16)
    return attend(query, key_value_cache, step_key_value, cache_valid_length)


def solution(mesh):
    return jax.shard_map(
        per_device,
        mesh=mesh,
        in_specs=(
            P(None, "dp", "tensor"),
            P(None, "tensor"),
            P("dp", "tensor"),
            P("dp", "tensor"),
            P(None, "dp", None, "tensor"),
            P(None, None, "dp", "tensor"),
            P("dp"),
            P("dp"),
            P(),
        ),
        out_specs=P(None, "dp", "tensor"),
        check_vma=False,
    )
```

profile of v0, /device:TPU:0, one launch (start us, length us, event | category | flops | bytes accessed | tf_op | source)
XLA Modules:
  0.0 223.6 jit_solution(11072860892309198961)
XLA Ops:
  6.5 0.7 all-gather.6.cloned.1.call-update
  7.3 0.7 all-gather.4.cloned.1.call-update
  8.1 0.7 all-gather.8.cloned.1.call-update
  8.8 0.8 select_reduce_fusion
  9.5 0.7 iota_compare_fusion
  10.3 0.9 fusion.56
  11.2 50.3 %all-gather.6.cloned.1.call-done = bf16[1024,1024]{1,0:T(8,128)(2,1)} async-done(((bf16[128,1024]{1,0:T(8,128)(2,1)}), bf16[1024,1024]{1,0:T(8,128)(2,1)}) %all-gather.6.cloned.1.call-update) | async-done | bytes 2097168 | tf_op jit(solution)/shard_map/all_gather | solution.py:94
  61.5 7.2 %gather_fusion = bf16[64,64,1024]{2,1,0:T(8,128)(2,1)} fusion(bf16[16,64,1024]{2,1,0:T(8,128)(2,1)} %bitcast.96, s32[1024]{0:T(1024)S(1)} %pad_clamp_fusion), kind=kCustom, calls=%fused_computation | custom fusion | bytes 16777472 | tf_op jit(solution)/shard_map/jit(_take)/gather | solution.py:97
  68.7 27.4 %all-gather.4.cloned.1.call-done = bf16[256,8192]{1,0:T(8,128)(2,1)} async-done(((bf16[256,2048]{1,0:T(8,128)(2,1)}), bf16[256,8192]{1,0:T(8,128)(2,1)}) %all-gather.4.cloned.1.call-update) | async-done | bytes 4194320 | tf_op jit(solution)/shard_map/all_gather | solution.py:88
  96.1 9.5 %fusion.59 = f32[256,1024]{1,0:T(8,128)S(1)} fusion(bf16[256,8192]{1,0:T(8,128)(2,1)} %all-gather.4.cloned.1.call-done, bf16[8192,1024]{1,0:T(8,128)(2,1)} %param.10), kind=kOutput, calls=%fused_computation.58 | convolution fusion | flops 4294967296 | bytes 22020096 | tf_op jit(solution)/shard_map/dot_general | solution.py:87
  105.6 66.1 %all-gather.8.cloned.1.call-done = bf16[1024,2048]{1,0:T(8,128)(2,1)} async-done(((bf16[128,2048]{1,0:T(8,128)(2,1)}), bf16[1024,2048]{1,0:T(8,128)(2,1)}) %all-gather.8.cloned.1.call-update) | async-done | bytes 4194320 | tf_op jit(solution)/shard_map/all_gather | solution.py:93
  171.6 9.8 %gather_fusion.1 = bf16[64,64,2048]{2,1,0:T(8,128)(2,1)} fusion(bf16[16,64,2048]{2,1,0:T(8,128)(2,1)} %bitcast.95, s32[1024]{0:T(1024)S(1)} %pad_clamp_fusion), kind=kCustom, calls=%fused_computation.1 | custom fusion | bytes 33554688 | tf_op jit(solution)/shard_map/jit(_take)/gather | solution.py:96
  181.5 8.1 %fusion.37 = f32[4,64,64]{2,0,1:T(4,128)S(1)} fusion(bf16[64,64,2048]{2,1,0:T(8,128)(2,1)} %gather_fusion.1, pred[64]{0:T(512)(128)(4,1)S(1)} %compare_and_fusion, bf16[4,64,2048]{2,1,0:T(8,128)(2,1)S(1)} %copy-done), kind=kOutput, calls=%fused_computation.27 | convolution fusion | flops 75497472 | bytes 17891392 | tf_op jit(solution)/shard_map/trd,rjd->trj/dot_general | solution.py:19
  189.6 11.7 %psum.7 = bf16[4,64,64]{2,0,1:T(4,128)(2,1)S(1)} all-reduce(f32[4,64,64]{2,0,1:T(4,128)S(1)} %fusion.37), channel_id=1, replica_groups=mesh['dp'=8,'tensor'=4] {'tensor'}, use_global_device_ids=true, to_apply=%region_1.2 | all-reduce | flops 16384 | bytes 98304 | tf_op jit(solution)/shard_map/psum | solution.py:22
  201.3 4.9 %fusion.27 = bf16[4,64,1024]{2,0,1:T(4,128)(2,1)S(1)} fusion(bf16[64,64,1024]{2,1,0:T(8,128)(2,1)} %gather_fusion, pred[64]{0:T(512)(128)(4,1)S(1)} %compare_and_fusion, f32[4,64,1024]{2,1,0:T(8,128)S(1)} %bitcast.98, bf16[4,64,64]{2,0,1:T(4,128)(2,1)S(1)} %psum.7), kind=kOutput, calls=%fused_computation.22 | convolution fusion | flops 38273024 | bytes 9994304 | tf_op jit(solution)/shard_map/trj,rjh->trh/dot_general | solution.py:23
  206.2 0.2 reshape.139
  206.4 2.4 %fusion.58 = (f32[4,64,8]{2,0,1:T(4,128)S(1)}, f32[4,64,1,8,4]{3,4,0,1,2:T(4,128)S(1)}) fusion(bf16[4,64,8,128]{3,2,0,1:T(8,128)(2,1)S(1)} %reshape.139, bf16[4,1,64,128]{3,2,1,0:T(8,128)(2,1)S(1)} %get-tuple-element.6, pred[4,4]{1,0:T(4,128)(4,1)S(1)} %iota_compare_fusion.2), kind=kOutput, calls=%fused_computation.57 | convolution fusion | flops 2119680 | bytes 630800 | tf_op jit(solution)/shard_map/trkgd,srkd->trkgs/dot_general | solution.py:44
  208.8 2.9 %fusion.57 = (f32[4,64,8]{2,0,1:T(4,128)S(1)}, f32[4,64,1,8,128]{4,3,0,1,2:T(8,128)S(1)}) fusion(bf16[4,64,8,128]{3,2,0,1:T(8,128)(2,1)S(1)} %reshape.139, bf16[2,64,128,128]{3,2,1,0:T(8,128)(2,1)} %param.13, pred[64,128]{1,0:T(8,128)(4,1)S(1)} %iota_compare_fusion), kind=kOutput, calls=%fused_computation.56 | convolution fusion | flops 67893248 | bytes 3686400 | tf_op jit(solution)/shard_map/trkgd,rckd->trkgc/dot_general | solution.py:39
  211.8 0.7 fusion.42
  212.5 2.3 %fusion.8 = f32[64,4,8,128]{3,2,1,0:T(8,128)S(1)} fusion(bf16[2,64,128,128]{3,2,1,0:T(8,128)(2,1)} %param.13, f32[4,64,1,8,128]{4,3,0,1,2:T(8,128)S(1)} %get-tuple-element.8, f32[4,64,8]{2,0,1:T(4,128)S(1)} %max.9), kind=kOutput, calls=%fused_computation.10 | convolution fusion | flops 67633152 | bytes 4202496 | tf_op jit(solution)/shard_map/trkgc,rckd->trkgd/dot_general | solution.py:55
  214.8 0.5 fusion.47
  215.4 0.6 divide_convert_fusion
  216.0 0.1 convert_element_type.23
  216.1 1.0 copy.17
  (11 shorter events, 0.2 us)
Async XLA Ops:
  6.5 55.0 %all-gather.6.cloned.1.call-start = ((), (), s32[]{:S(2)}) async-start(), calls=%async_computation.1 | async-start | bytes 2359296 | tf_op jit(solution)/shard_map/all_gather | solution.py:94
  7.3 88.8 %all-gather.4.cloned.1.call-start = ((), (), s32[]{:S(2)}) async-start(), calls=%async_computation | async-start | bytes 5242880 | tf_op jit(solution)/shard_map/all_gather | solution.py:88
  8.0 163.6 %all-gather.8.cloned.1.call-start = ((), (), s32[]{:S(2)}) async-start(), calls=%async_computation.2 | async-start | bytes 4718592 | tf_op jit(solution)/shard_map/all_gather | solution.py:93
  171.6 9.8 %copy-start = (bf16[4,64,2048]{2,1,0:T(8,128)(2,1)S(1)}, bf16[4,64,2048]{2,1,0:T(8,128)(2,1)}, u32[]{:S(2)}) copy-start(bf16[4,64,2048]{2,1,0:T(8,128)(2,1)} %param.9) | copy-start | bytes 3145732
Sparse Core Ops, SparseCore 0:
  9.5 51.9 all-gather.5
  63.1 32.9 all-gather.3
  98.2 73.3 all-gather.7
where the time goes:
time: 224 us
  waiting for transfers between devices  146 us (65%)
  matrix products  30.8 us (14%)
  local copies, waits for them, and re-layouts  19.2 us (9%)
  between operations  13.2 us (6%)
  blocking collectives  11.7 us (5%)
  other arithmetic  2.82 us (1%)
    all_gather x1, waiting for transfers between devices, per_device(): lax.all_gather(adapter_down_maps, 'dp', axis=0, tiled=True)  66.1 us
    all_gather x1, waiting for transfers between devices, per_device(): lax.all_gather(adapter_up_maps, 'dp', axis=0, tiled=True)  50.3 us
    all_gather x1, waiting for transfers between devices, per_device(): lax.all_gather(token_rows, 'tensor', axis=1, tiled=True)  27.4 us
    psum x1, blocking collectives, adapt_rows(): shrink = lax.psum(shrink_local, 'tensor').astype(jnp.bfloat16)  11.7 us
    gather x1, local copies, waits for them, and re-layouts, per_device(): jnp.take(down_all.reshape(-1, ADAPTER_RANK, part_width), position, axis=0)  9.82 us
    dot_general x1, matrix products, per_device(): jnp.dot(lax.all_gather(token_rows, 'tensor', axis=1, tiled=True), query_p...  9.48 us
    dot_general x1, matrix products, adapt_rows(): jnp.einsum('trd,rjd->trj', normed_hidden_state, down_map_pages, preferred...  8.13 us
    gather x1, local copies, waits for them, and re-layouts, per_device(): jnp.take(up_all.reshape(-1, ADAPTER_RANK, heads_width), position, axis=0)  7.17 us
  transfers between devices with their start and end apart: 3, of which 3 were waited for; matrix products, arithmetic and copies ran while one was open for 9% of the time, Pallas kernels for 0%

commit v1 on v0

v1 whole, which is shorter than its diff:
```python
import functools
import math

import jax
import jax.numpy as jnp
from jax import lax
from jax.experimental import pallas as pl
from jax.experimental.pallas import tpu as pltpu
from jax.sharding import PartitionSpec as P

HEAD_SIZE = 128
ADAPTER_RANK = 64
MESH = pl.DeviceIdType.MESH
F32 = jnp.float32
BF16 = jnp.bfloat16


def project_kernel(
    line,
    hid_hbm,
    w_hbm,
    down_hbm,
    up_hbm,
    pos_hbm,
    query_ref,
    hid,
    rows_x,
    pos,
    downs,
    ups,
    w,
    acc,
    part,
    got,
    local_sem,
    w_sem,
    h1_s,
    h1_r,
    h2_s,
    h2_r,
    hf_s,
    hf_r,
    x_s,
    x_r,
    zd_s,
    zd_r,
    zu_s,
    zu_r,
    xu_s,
    xu_r,
    red_s,
    red_r,
):
    d = lax.axis_index("dp")
    t = lax.axis_index("tensor")
    q, p = d // 2, d % 2
    other = 1 - p
    t1 = t + 1 - 2 * (t % 2)
    t2 = (t + 2) % 4
    t3 = (t1 + 2) % 4
    above, below, across = (d + 2, t), (d - 2, t), (d + 1 - 2 * p, t)
    side1, side2 = (d, t1), (d, t2)
    count = hid.shape[1]
    width = hid.shape[2]
    chunk = count // 4
    out_cols = w.shape[1]
    has_above, has_below = q < line - 1, q > 0

    def local(src, dst, k):
        return pltpu.make_async_copy(src, dst, local_sem.at[k])

    def remote(src, dst, s, r, to):
        return pltpu.make_async_remote_copy(
            src_ref=src, dst_ref=dst, send_sem=s, recv_sem=r, device_id=to, device_id_type=MESH
        )

    first = [
        local(down_hbm, downs.at[q], 0),
        local(hid_hbm, hid.at[t], 1),
        local(pos_hbm, pos.at[0], 2),
        local(up_hbm, ups.at[p, q], 3),
    ]
    for c in first:
        c.start()
    order = [t, t1, t2, t3]
    w_copies = []
    for k, block in enumerate(order):
        span = pl.ds(pl.multiple_of(block * width, width), width)
        w_copies.append(pltpu.make_async_copy(w_hbm.at[span], w.at[span], w_sem.at[k]))
        w_copies[-1].start()

    barrier = pltpu.get_barrier_semaphore()
    for peer in (across, side1, side2):
        pl.semaphore_signal(barrier, inc=1, device_id=peer, device_id_type=MESH)

    @pl.when(has_above)
    def _():
        pl.semaphore_signal(barrier, inc=1, device_id=above, device_id_type=MESH)

    @pl.when(has_below)
    def _():
        pl.semaphore_signal(barrier, inc=1, device_id=below, device_id_type=MESH)

    pl.semaphore_wait(
        barrier, 3 + jnp.where(has_above, 1, 0) + jnp.where(has_below, 1, 0)
    )
    for c in first:
        c.wait()

    def line_copy(kind, way, s, slot):
        ref = downs.at[slot] if kind == 0 else ups.at[p, slot]
        send, recv = (zd_s, zd_r) if kind == 0 else (zu_s, zu_r)
        return remote(
            ref, ref, send.at[way, s], recv.at[way, s], above if way == 0 else below
        )

    def sends(way, s):
        if way == 0:
            return jnp.logical_and(has_above, q - s >= 0)
        return jnp.logical_and(has_below, q + s <= line - 1)

    def sent_slot(way, s):
        return q - s if way == 0 else q + s

    def arrives(way, s):
        return q - 1 - s >= 0 if way == 0 else q + 1 + s <= line - 1

    def arrived_slot(way, s):
        return q - 1 - s if way == 0 else q + 1 + s

    def send_line(kind, way, s):
        @pl.when(sends(way, s))
        def _():
            line_copy(kind, way, s, sent_slot(way, s)).start()

    def cross_copy(index, slot, parity):
        ref = ups.at[parity, slot]
        return remote(ref, ref, xu_s.at[index], xu_r.at[index], across)

    x_rows = remote(hid.at[t], rows_x, x_s.at[0], x_r.at[0], across)
    x_pos = remote(pos.at[0], pos.at[1], x_s.at[1], x_r.at[1], across)
    to1 = remote(hid.at[t], hid.at[t], h1_s, h1_r, side1)

    def part_of(block, c):
        return hid.at[block, pl.ds(c * chunk, chunk)]

    to2 = [
        remote(part_of(t, c), part_of(t, c), h2_s.at[c], h2_r.at[c], side2) for c in range(4)
    ]
    from2 = [
        remote(part_of(t2, c), part_of(t2, c), h2_s.at[c], h2_r.at[c], side2) for c in range(4)
    ]
    on1 = [
        remote(part_of(t2, c), part_of(t2, c), hf_s.at[c], hf_r.at[c], side1) for c in range(4)
    ]
    by1 = [
        remote(part_of(t3, c), part_of(t3, c), hf_s.at[c], hf_r.at[c], side1) for c in range(4)
    ]
    send_line(0, 0, 0)
    send_line(0, 1, 0)
    for c in to2:
        c.start()
    x_pos.start()
    x_rows.start()
    to1.start()
    send_line(1, 0, 0)
    send_line(1, 1, 0)
    cross_copy(q, q, p).start()

    tile = 256

    def base(block, k, start):
        w_copies[k].wait()
        span = pl.ds(pl.multiple_of(block * width, width), width)

        @pl.loop(0, out_cols // tile)
        def _(n):
            cols = pl.ds(pl.multiple_of(n * tile, tile), tile)
            value = jnp.dot(hid[block], w[span, cols], preferred_element_type=F32)
            if start:
                acc[:, cols] = value
            else:
                acc[:, cols] += value

    half = lax.broadcasted_iota(jnp.int32, (count // 4, 2 * ADAPTER_RANK), 1) // ADAPTER_RANK

    def keep(which, wanted):
        m = jnp.where(wanted, 1, 0)
        return jnp.concatenate([m] * 4, axis=0) > 0

    def shrink(which, slot, start=False):
        source = hid[t] if which == 0 else rows_x[...]
        value = lax.dot_general(
            source, downs[slot], (((1,), (1,)), ((), ())), preferred_element_type=F32
        )
        value = jnp.where(
            keep(which, pos[which] == 2 * (2 * slot + p) + half), value, 0.0
        )
        if start:
            part[which] = value
        else:
            part[which] += value

    base(t, 0, True)
    shrink(0, q, True)

    def pass_on(c):
        from2[c].wait_recv()
        on1[c].start()

    def down_step(s):
        for way in (0, 1):

            @pl.when(arrives(way, s))
            def _():
                line_copy(0, way, s, arrived_slot(way, s)).wait_recv()

            if s + 1 < line:
                send_line(0, way, s + 1)

    def down_use(which, s):
        for way in (0, 1):

            @pl.when(arrives(way, s))
            def _():
                shrink(which, arrived_slot(way, s))

    def up_step(s):
        for way in (0, 1):

            @pl.when(arrives(way, s))
            def _():
                slot = arrived_slot(way, s)
                line_copy(1, way, s, slot).wait_recv()
                cross_copy(slot, slot, p).start()

            if s + 1 < line:
                send_line(1, way, s + 1)

    pass_on(0)
    pass_on(1)
    down_step(0)
    down_use(0, 0)
    pass_on(2)
    up_step(0)
    pass_on(3)
    to1.wait_recv()
    base(t1, 1, False)
    x_pos.wait_recv()
    x_rows.wait_recv()
    shrink(1, q, True)
    down_use(1, 0)
    base(t2, 2, False)
    for s in range(1, line - 1):
        down_step(s)
        down_use(0, s)
        down_use(1, s)
        if s == 1:
            for c in by1:
                c.wait_recv()
            base(t3, 3, False)
        if s < line - 2:
            up_step(s)

    to_x = remote(part.at[1], got.at[0], red_s.at[0], red_r.at[0], across)
    to_x.start()
    to_x.wait_recv()
    part[0] += got[0]
    to_1 = remote(part.at[0], got.at[1], red_s.at[1], red_r.at[1], side1)
    to_1.start()
    to_1.wait_recv()
    part[2] = part[0] + got[1]
    to_2 = remote(part.at[2], got.at[2], red_s.at[2], red_r.at[2], side2)
    to_2.start()
    up_step(line - 2)
    to_2.wait_recv()
    total = (part[2] + got[2]).astype(BF16)

    def expand(parity, last):
        picked = jnp.concatenate(
            [
                jnp.where(keep(0, pos[0] // 2 == 2 * slot + parity), total, jnp.zeros_like(total))
                for slot in range(line)
            ],
            axis=1,
        )

        @pl.loop(0, out_cols // tile)
        def _(n):
            cols = pl.ds(pl.multiple_of(n * tile, tile), tile)
            maps = ups[parity, :, :, cols].reshape(line * 2 * ADAPTER_RANK, tile)
            value = acc[:, cols] + jnp.dot(picked, maps, preferred_element_type=F32)
            if last:
                query_ref[:, cols] = value.astype(BF16)
            else:
                acc[:, cols] = value

    expand(p, False)
    for slot in range(line):
        cross_copy(slot, slot, other).wait_recv()
    expand(other, True)

    x_rows.wait_send()
    x_pos.wait_send()
    to1.wait_send()
    for c in to2 + on1:
        c.wait_send()
    for c in (to_x, to_1, to_2):
        c.wait_send()
    for slot in range(line):
        cross_copy(slot, slot, p).wait_send()
    for s in range(line):
        for way in (0, 1):

            @pl.when(sends(way, s))
            def _():
                slot = sent_slot(way, s)
                line_copy(0, way, s, slot).wait_send()
                line_copy(1, way, s, slot).wait_send()


def project(token_rows, weight, down, up, position, line):
    count, width = token_rows.shape
    cols = weight.shape[1]
    pages = 2 * ADAPTER_RANK
    anywhere = pl.BlockSpec(memory_space=pl.ANY)
    sems = pltpu.SemaphoreType.DMA
    return pl.pallas_call(
        functools.partial(project_kernel, line),
        out_shape=jax.ShapeDtypeStruct((count, cols), BF16),
        in_specs=[anywhere] * 5,
        out_specs=pl.BlockSpec(memory_space=pltpu.VMEM),
        scratch_shapes=[
            pltpu.VMEM((4, count, width), BF16),
            pltpu.VMEM((count, width), BF16),
            pltpu.VMEM((2, count // 4, pages), jnp.int32),
            pltpu.VMEM((line, pages, width), BF16),
            pltpu.VMEM((2, line, pages, cols), BF16),
            pltpu.VMEM(weight.shape, BF16),
            pltpu.VMEM((count, cols), F32),
            pltpu.VMEM((3, count, pages), F32),
            pltpu.VMEM((3, count, pages), F32),
            sems((4,)),
            sems((4,)),
            sems,
            sems,
            sems((4,)),
            sems((4,)),
            sems((4,)),
            sems((4,)),
            sems((2,)),
            sems((2,)),
            sems((2, line)),
            sems((2, line)),
            sems((2, line)),
            sems((2, line)),
            sems((line,)),
            sems((line,)),
            sems((3,)),
            sems((3,)),
        ],
        compiler_params=pltpu.CompilerParams(
            collective_id=0, has_side_effects=True, vmem_limit_bytes=56 * 2**20
        ),
    )(token_rows, weight, down, up, position)


def attend_kernel(steps, q_ref, k_ref, v_ref, nk_ref, nv_ref, len_ref, out_ref):
    q = q_ref[...]
    scale = 1.0 / math.sqrt(HEAD_SIZE)
    dims = (((2,), (2,)), ((0,), (0,)))
    cached = lax.dot_general(q, k_ref[0], dims, preferred_element_type=F32) * scale
    fresh = lax.dot_general(q, nk_ref[...], dims, preferred_element_type=F32) * scale
    place = lax.broadcasted_iota(jnp.int32, cached.shape, 2)
    cached = jnp.where(place < len_ref[...], cached, -1e30)
    step = lax.broadcasted_iota(jnp.int32, fresh.shape, 1) // (q.shape[1] // steps)
    fresh = jnp.where(lax.broadcasted_iota(jnp.int32, fresh.shape, 2) <= step, fresh, -1e30)
    top = jnp.maximum(
        jnp.max(cached, axis=-1, keepdims=True), jnp.max(fresh, axis=-1, keepdims=True)
    )
    cached = jnp.exp(cached - top)
    fresh = jnp.exp(fresh - top)
    total = jnp.sum(cached, axis=-1, keepdims=True) + jnp.sum(fresh, axis=-1, keepdims=True)
    dims = (((2,), (1,)), ((0,), (0,)))
    mixed = lax.dot_general(cached.astype(BF16), v_ref[0], dims, preferred_element_type=F32)
    mixed += lax.dot_general(fresh.astype(BF16), nv_ref[...], dims, preferred_element_type=F32)
    out_ref[...] = (mixed / total).astype(BF16)


def attend(query, cache, fresh, lengths, steps):
    requests, rows, size = query.shape
    length = cache.shape[2]
    pad = fresh.shape[2]
    block = 8

    def spec(which, n):
        return pl.BlockSpec((1, block, n, size), lambda i: (which, i, 0, 0))

    def plain(n):
        return pl.BlockSpec((block, n, size), lambda i: (i, 0, 0))

    return pl.pallas_call(
        functools.partial(attend_kernel, steps),
        grid=(requests // block,),
        out_shape=jax.ShapeDtypeStruct(query.shape, BF16),
        in_specs=[
            plain(rows),
            spec(0, length),
            spec(1, length),
            plain(pad),
            plain(pad),
            plain(1),
        ],
        out_specs=plain(rows),
        compiler_params=pltpu.CompilerParams(vmem_limit_bytes=32 * 2**20),
    )(query, cache, cache, fresh[0], fresh[1], lengths)


def per_device(line, hidden, weight, down, up, cache, step_kv, valid, adapters, pool):
    steps, requests, width = hidden.shape
    table = jnp.arange(pool.shape[0], dtype=jnp.int32)
    position = jnp.sum(jnp.where(adapters[:, None] == table[None, :], pool[None, :], 0), axis=1)
    position = jnp.broadcast_to(position[:, None], (requests, 2 * ADAPTER_RANK))
    query = project(hidden.reshape(steps * requests, width), weight, down, up, position, line)
    heads = weight.shape[1] // HEAD_SIZE
    query = query.reshape(steps, requests, heads, HEAD_SIZE).transpose(1, 0, 2, 3)
    fresh = jnp.pad(step_kv.transpose(1, 2, 0, 3), ((0, 0), (0, 0), (0, 16 - steps), (0, 0)))
    lengths = jnp.broadcast_to(valid[:, None, None], (requests, 1, HEAD_SIZE))
    out = attend(
        query.reshape(requests, steps * heads, HEAD_SIZE), cache, fresh, lengths, steps
    )
    out = out.reshape(requests, steps, heads * HEAD_SIZE)
    return out.transpose(1, 0, 2)


def solution(mesh):
    return jax.shard_map(
        functools.partial(per_device, mesh.shape["dp"] // 2),
        mesh=mesh,
        in_specs=(
            P(None, "dp", "tensor"),
            P(None, "tensor"),
            P("dp", "tensor"),
            P("dp", "tensor"),
            P(None, "dp", None, "tensor"),
            P(None, None, "dp", "tensor"),
            P("dp"),
            P("dp"),
            P(),
        ),
        out_specs=P(None, "dp", "tensor"),
        check_vma=False,
    )
```

time: 224 us -> 80.9 us (0.36)
  waiting for transfers between devices: 146 us -> 0 us
  Pallas kernels: 0 us -> 74.9 us
  matrix products: 30.8 us -> 0 us
  local copies, waits for them, and re-layouts: 19.2 us -> 4.87 us
  between operations: 13.2 us -> 0.07 us
  blocking collectives: 11.7 us -> 0 us
    all_gather x3 -> x0, waiting for transfers between devices: 144 us -> none  [the longest x1 66.1 us: per_device(): lax.all_gather(adapter_down_maps, 'dp', axis=0, tiled=True)]
    pallas_call x0 -> x2, Pallas kernels: none -> 74.9 us  [the longest x1 70.2 us: project(): pl.pallas_call(functools.partial(project_kernel, line), out_shape=jax.Sha...]
    dot_general x7 -> x0, matrix products: 30.8 us -> none  [the longest x1 9.48 us: per_device(): jnp.dot(lax.all_gather(token_rows, 'tensor', axis=1, tiled=True), query_p...]
    gather x2 -> x0, local copies, waits for them, and re-layouts: 17 us -> none  [the longest x1 9.82 us: per_device(): jnp.take(down_all.reshape(-1, ADAPTER_RANK, part_width), position, axis=0)]
    psum x1 -> x0, blocking collectives: 11.7 us -> none  [adapt_rows(): shrink = lax.psum(shrink_local, 'tensor').astype(jnp.bfloat16)]
  transfers between devices with their start and end apart: 3 -> 0, of which waited for: 3 -> 0; matrix products, arithmetic and copies ran while one was open for 9% -> 0% of each run, Pallas kernels for 0% -> 0%
where the time goes in v1:
time: 80.9 us; the launch traced here: 80.7 us
  Pallas kernels  74.9 us (93%)
  local copies, waits for them, and re-layouts  4.87 us (6%)
  other arithmetic  0.91 us (1%)
    pallas_call x1, Pallas kernels, project(): pl.pallas_call(functools.partial(project_kernel, line), out_shape=jax.Sha...  70.2 us
    pallas_call x1, Pallas kernels, attend(): pl.pallas_call(functools.partial(attend_kernel, steps), grid=(requests //...  4.67 us
    unnamed x4, local copies, waits for them, and re-layouts  2.15 us

profile of v1, /device:TPU:0, one launch (start us, length us, event | category | flops | bytes accessed | tf_op | source)
XLA Modules:
  0.0 80.7 jit_solution(8502801669631160094)
XLA Ops:
  0.0 0.0 copy-start
  0.0 0.9 %select_reduce_fusion = s32[64]{0:T(128)S(1)} fusion(s32[16]{0:T(128)} %param.17, s32[64]{0:T(128)} %param.16), kind=kLoop, calls=%fused_computation.7 | loop fusion | flops 3008 | bytes 576 | tf_op jit(solution)/shard_map/reduce_sum | solution.py:422
  0.9 0.7 broadcast_in_dim.18.pos_hbm
  1.6 0.8 broadcast_in_dim.30.len_ref
  2.4 1.0 %copy.21 = bf16[4,2,64,128]{3,0,2,1:T(4,128)(2,1)S(1)} copy(bf16[4,2,64,128]{3,2,1,0:T(8,128)(2,1)} %param.14) | data formatting | bytes 262144 | tf_op args[5]
  3.4 0.1 fusion.1
  3.5 70.2 %shard_map.91 = bf16[256,1024]{1,0:T(8,128)(2,1)} custom-call(bf16[256,2048]{1,0:T(8,128)(2,1)} %bitcast.24, bf16[8192,1024]{1,0:T(8,128)(2,1)} %w_hbm.1, bf16[128,2048]{1,0:T(8,128)(2,1)} %down_hbm.1, bf16[128,1024]{1,0:T(8,128)(2,1)} %up_hbm.1, s32[64,128]{1,0:T(8,128)} %broadcast_in_dim.18.pos_hbm), custom_call_target="tpu_custom_call" | custom-call | tf_op jit(solution)/shard_map/pallas_call | solution.py:328
  73.7 1.1 %copy.16 = bf16[32,8,8,128]{3,2,1,0:T(8,128)(2,1)S(1)} copy(bf16[32,8,8,128]{3,1,2,0:T(8,128)(2,1)} %bitcast.22) | data formatting | bytes 1048576
  74.9 0.1 copy_bitcast_fusion.1.q_ref
  75.0 0.0 copy-done
  75.0 4.7 %shard_map.92 = bf16[64,32,128]{2,1,0:T(8,128)(2,1)S(1)} custom-call(bf16[64,32,128]{2,1,0:T(8,128)(2,1)S(1)} %copy_bitcast_fusion.1.q_ref, bf16[2,64,128,128]{3,2,1,0:T(8,128)(2,1)S(1)} %copy-done, bf16[2,64,128,128]{3,2,1,0:T(8,128)(2,1)S(1)} %copy-done, bf16[64,16,128]{2,1,0:T(8,128)(2,1)S(1)} %get-tuple-element.6.nk_ref, ...), custom_call_target="tpu_custom_call" | custom-call | tf_op jit(solution)/shard_map/pallas_call | solution.py:402
  79.7 0.1 reshape.21
  79.8 1.0 %copy.20 = bf16[64,4,1024]{2,0,1:T(8,128)(2,1)} copy(bf16[64,4,1024]{2,1,0:T(4,128)(2,1)S(1)} %reshape.21) | data formatting | bytes 1048576 | tf_op jit(solution)/shard_map/reshape | solution.py:432
Async XLA Ops:
  0.0 75.0 %copy-start = (bf16[2,64,128,128]{3,2,1,0:T(8,128)(2,1)S(1)}, bf16[2,64,128,128]{3,2,1,0:T(8,128)(2,1)}, u32[]{:S(2)}) copy-start(bf16[2,64,128,128]{3,2,1,0:T(8,128)(2,1)} %v_ref.1) | copy-start | bytes 12582916

commit v2 on v1

--- a/solution.py
+++ b/solution.py
@@ -28,9 +28,12 @@
     pos,
     downs,
     ups,
+    picks,
+    ups_x,
     w,
     acc,
     part,
+    packed,
     got,
     local_sem,
     w_sem,
@@ -78,7 +81,7 @@
         local(down_hbm, downs.at[q], 0),
         local(hid_hbm, hid.at[t], 1),
         local(pos_hbm, pos.at[0], 2),
-        local(up_hbm, ups.at[p, q], 3),
+        local(up_hbm, ups.at[q], 3),
     ]
     for c in first:
         c.start()
@@ -108,7 +111,7 @@
         c.wait()
 
     def line_copy(kind, way, s, slot):
-        ref = downs.at[slot] if kind == 0 else ups.at[p, slot]
+        ref = downs.at[slot] if kind == 0 else ups.at[slot]
         send, recv = (zd_s, zd_r) if kind == 0 else (zu_s, zu_r)
         return remote(
             ref, ref, send.at[way, s], recv.at[way, s], above if way == 0 else below
@@ -133,9 +136,21 @@
         def _():
             line_copy(kind, way, s, sent_slot(way, s)).start()
 
-    def cross_copy(index, slot, parity):
-        ref = ups.at[parity, slot]
-        return remote(ref, ref, xu_s.at[index], xu_r.at[index], across)
+    def cross_copy(slot):
+        return remote(picks.at[slot], ups_x.at[slot], xu_s.at[slot], xu_r.at[slot], across)
+
+    def cross(slot):
+        second = jnp.where(pos[1] == 2 * (2 * slot + p) + 1, 1.0, 0.0)
+        second = jnp.max(second, axis=0, keepdims=True)
+        second = jnp.broadcast_to(second, (ADAPTER_RANK, second.shape[1])) > 0.5
+        for c in range(0, out_cols, 2 * ADAPTER_RANK):
+            cols = pl.ds(c, 2 * ADAPTER_RANK)
+            picks[slot, :, cols] = jnp.where(
+                second,
+                ups[slot, pl.ds(ADAPTER_RANK, ADAPTER_RANK), cols],
+                ups[slot, pl.ds(0, ADAPTER_RANK), cols],
+            )
+        cross_copy(slot).start()
 
     x_rows = remote(hid.at[t], rows_x, x_s.at[0], x_r.at[0], across)
     x_pos = remote(pos.at[0], pos.at[1], x_s.at[1], x_r.at[1], across)
@@ -156,16 +171,15 @@
     by1 = [
         remote(part_of(t3, c), part_of(t3, c), hf_s.at[c], hf_r.at[c], side1) for c in range(4)
     ]
+    x_pos.start()
     send_line(0, 0, 0)
     send_line(0, 1, 0)
     for c in to2:
         c.start()
-    x_pos.start()
     x_rows.start()
     to1.start()
     send_line(1, 0, 0)
     send_line(1, 1, 0)
-    cross_copy(q, q, p).start()
 
     tile = 256
 
@@ -201,6 +215,8 @@
         else:
             part[which] += value
 
+    x_pos.wait_recv()
+    cross(q)
     base(t, 0, True)
     shrink(0, q, True)
 
@@ -232,7 +248,7 @@
             def _():
                 slot = arrived_slot(way, s)
                 line_copy(1, way, s, slot).wait_recv()
-                cross_copy(slot, slot, p).start()
+                cross(slot)
 
             if s + 1 < line:
                 send_line(1, way, s + 1)
@@ -246,7 +262,6 @@
     pass_on(3)
     to1.wait_recv()
     base(t1, 1, False)
-    x_pos.wait_recv()
     x_rows.wait_recv()
     shrink(1, q, True)
     down_use(1, 0)
@@ -262,43 +277,60 @@
         if s < line - 2:
             up_step(s)
 
-    to_x = remote(part.at[1], got.at[0], red_s.at[0], red_r.at[0], across)
+    rank = ADAPTER_RANK
+    fold = count // 2
+    left = lax.broadcasted_iota(jnp.int32, (fold, 2 * rank), 1) < rank
+
+    def pack(value):
+        both = value + pltpu.roll(value, rank, 1)
+        return jnp.where(left, both[:fold], both[fold:])
+
+    def unpack(value):
+        turned = pltpu.roll(value, rank, 1)
+        return jnp.concatenate(
+            [jnp.where(left, value, turned), jnp.where(left, turned, value)], axis=0
+        )
+
+    packed[0] = pack(part[1])
+    to_x = remote(packed.at[0], got.at[0], red_s.at[0], red_r.at[0], across)
     to_x.start()
+    mine = pack(part[0])
     to_x.wait_recv()
-    part[0] += got[0]
-    to_1 = remote(part.at[0], got.at[1], red_s.at[1], red_r.at[1], side1)
+    packed[1] = mine + got[0]
+    to_1 = remote(packed.at[1], got.at[1], red_s.at[1], red_r.at[1], side1)
     to_1.start()
     to_1.wait_recv()
-    part[2] = part[0] + got[1]
-    to_2 = remote(part.at[2], got.at[2], red_s.at[2], red_r.at[2], side2)
+    packed[2] = packed[1] + got[1]
+    to_2 = remote(packed.at[2], got.at[2], red_s.at[2], red_r.at[2], side2)
     to_2.start()
     up_step(line - 2)
     to_2.wait_recv()
-    total = (part[2] + got[2]).astype(BF16)
-
-    def expand(parity, last):
-        picked = jnp.concatenate(
-            [
-                jnp.where(keep(0, pos[0] // 2 == 2 * slot + parity), total, jnp.zeros_like(total))
-                for slot in range(line)
-            ],
-            axis=1,
-        )
-
+    total = unpack(packed[2] + got[2]).astype(BF16)
+    nothing = jnp.zeros_like(total)
+
+    def expand(picked, maps_ref, last):
         @pl.loop(0, out_cols // tile)
         def _(n):
             cols = pl.ds(pl.multiple_of(n * tile, tile), tile)
-            maps = ups[parity, :, :, cols].reshape(line * 2 * ADAPTER_RANK, tile)
+            maps = maps_ref[:, :, cols].reshape(picked.shape[1], tile)
             value = acc[:, cols] + jnp.dot(picked, maps, preferred_element_type=F32)
             if last:
                 query_ref[:, cols] = value.astype(BF16)
             else:
                 acc[:, cols] = value
 
-    expand(p, False)
+    own = [
+        jnp.where(keep(0, pos[0] == 2 * (2 * slot + p) + half), total, nothing)
+        for slot in range(line)
+    ]
+    expand(jnp.concatenate(own, axis=1), ups, False)
     for slot in range(line):
-        cross_copy(slot, slot, other).wait_recv()
-    expand(other, True)
+        cross_copy(slot).wait_recv()
+    theirs = [
+        jnp.where(keep(0, pos[0] // 2 == 2 * (slot + half) + other), total, nothing)
+        for slot in range(0, line, 2)
+    ]
+    expand(jnp.concatenate(theirs, axis=1), ups_x, True)
 
     x_rows.wait_send()
     x_pos.wait_send()
@@ -308,7 +340,7 @@
     for c in (to_x, to_1, to_2):
         c.wait_send()
     for slot in range(line):
-        cross_copy(slot, slot, p).wait_send()
+        cross_copy(slot).wait_send()
     for s in range(line):
         for way in (0, 1):
 
@@ -335,11 +367,14 @@
             pltpu.VMEM((count, width), BF16),
             pltpu.VMEM((2, count // 4, pages), jnp.int32),
             pltpu.VMEM((line, pages, width), BF16),
-            pltpu.VMEM((2, line, pages, cols), BF16),
+            pltpu.VMEM((line, pages, cols), BF16),
+            pltpu.VMEM((line, pages // 2, cols), BF16),
+            pltpu.VMEM((line, pages // 2, cols), BF16),
             pltpu.VMEM(weight.shape, BF16),
             pltpu.VMEM((count, cols), F32),
-            pltpu.VMEM((3, count, pages), F32),
-            pltpu.VMEM((3, count, pages), F32),
+            pltpu.VMEM((2, count, pages), F32),
+            pltpu.VMEM((3, count // 2, pages), F32),
+            pltpu.VMEM((3, count // 2, pages), F32),
             sems((4,)),
             sems((4,)),
             sems,

time: 80.9 us -> 76.6 us (0.947)
  Pallas kernels: 74.9 us -> 70.6 us
    pallas_call x1, Pallas kernels: 70.2 us -> 65.9 us  [project(): pl.pallas_call(functools.partial(project_kernel, line), out_shape=jax.Sha...]
where the time goes in v2:
time: 76.6 us; the launch traced here: 76.5 us
  Pallas kernels  70.6 us (92%)
  local copies, waits for them, and re-layouts  4.87 us (6%)
  other arithmetic  0.91 us (1%)
    pallas_call x1, Pallas kernels, project(): pl.pallas_call(functools.partial(project_kernel, line), out_shape=jax.Sha...  65.9 us
    pallas_call x1, Pallas kernels, attend(): pl.pallas_call(functools.partial(attend_kernel, steps), grid=(requests //...  4.67 us
    unnamed x4, local copies, waits for them, and re-layouts  2.15 us

profile of v2, /device:TPU:0, one launch (start us, length us, event | category | flops | bytes accessed | tf_op | source)
XLA Modules:
  0.0 76.5 jit_solution(9706337142097298617)
XLA Ops:
  0.0 0.0 copy-start
  0.0 0.9 %select_reduce_fusion = s32[64]{0:T(128)S(1)} fusion(s32[16]{0:T(128)} %param.17, s32[64]{0:T(128)} %param.16), kind=kLoop, calls=%fused_computation.7 | loop fusion | flops 3008 | bytes 576 | tf_op jit(solution)/shard_map/reduce_sum | solution.py:457
  0.9 0.7 broadcast_in_dim.18.pos_hbm
  1.6 0.8 %broadcast_in_dim.30.len_ref = s32[64,1,128]{2,1,0:T(1,128)S(1)} broadcast(s32[64]{0:T(128)} %param.15), dimensions={0} | broadcast | bytes 33024 | tf_op jit(solution)/shard_map/broadcast_in_dim | solution.py:463
  2.4 1.0 %copy.21 = bf16[4,2,64,128]{3,0,2,1:T(4,128)(2,1)S(1)} copy(bf16[4,2,64,128]{3,2,1,0:T(8,128)(2,1)} %param.14) | data formatting | bytes 262144 | tf_op args[5]
  3.4 0.1 fusion.1
  3.5 65.9 %shard_map.91 = bf16[256,1024]{1,0:T(8,128)(2,1)} custom-call(bf16[256,2048]{1,0:T(8,128)(2,1)} %bitcast.24, bf16[8192,1024]{1,0:T(8,128)(2,1)} %w_hbm.1, bf16[128,2048]{1,0:T(8,128)(2,1)} %down_hbm.1, bf16[128,1024]{1,0:T(8,128)(2,1)} %up_hbm.1, s32[64,128]{1,0:T(8,128)} %broadcast_in_dim.18.pos_hbm), custom_call_target="tpu_custom_call" | custom-call | tf_op jit(solution)/shard_map/pallas_call | solution.py:360
  69.4 1.1 %copy.16 = bf16[32,8,8,128]{3,2,1,0:T(8,128)(2,1)S(1)} copy(bf16[32,8,8,128]{3,1,2,0:T(8,128)(2,1)} %bitcast.22) | data formatting | bytes 1048576
  70.6 0.1 copy_bitcast_fusion.1.q_ref
  70.7 0.0 copy-done
  70.7 4.7 %shard_map.92 = bf16[64,32,128]{2,1,0:T(8,128)(2,1)S(1)} custom-call(bf16[64,32,128]{2,1,0:T(8,128)(2,1)S(1)} %copy_bitcast_fusion.1.q_ref, bf16[2,64,128,128]{3,2,1,0:T(8,128)(2,1)S(1)} %copy-done, bf16[2,64,128,128]{3,2,1,0:T(8,128)(2,1)S(1)} %copy-done, bf16[64,16,128]{2,1,0:T(8,128)(2,1)S(1)} %get-tuple-element.6.nk_ref, ...), custom_call_target="tpu_custom_call" | custom-call | tf_op jit(solution)/shard_map/pallas_call | solution.py:437
  75.4 0.1 reshape.21
  75.5 1.0 %copy.20 = bf16[64,4,1024]{2,0,1:T(8,128)(2,1)} copy(bf16[64,4,1024]{2,1,0:T(4,128)(2,1)S(1)} %reshape.21) | data formatting | bytes 1048576 | tf_op jit(solution)/shard_map/reshape | solution.py:467
Async XLA Ops:
  0.0 70.7 %copy-start = (bf16[2,64,128,128]{3,2,1,0:T(8,128)(2,1)S(1)}, bf16[2,64,128,128]{3,2,1,0:T(8,128)(2,1)}, u32[]{:S(2)}) copy-start(bf16[2,64,128,128]{3,2,1,0:T(8,128)(2,1)} %v_ref.1) | copy-start | bytes 12582916

commit v3 on v2

--- a/solution.py
+++ b/solution.py
@@ -53,6 +53,13 @@
     xu_r,
     red_s,
     red_r,
+    far,
+    far_pos,
+    far_part,
+    far_pack,
+    far_got,
+    far_s,
+    far_r,
 ):
     d = lax.axis_index("dp")
     t = lax.axis_index("tensor")
@@ -68,6 +75,11 @@
     chunk = count // 4
     out_cols = w.shape[1]
     has_above, has_below = q < line - 1, q > 0
+    near = width - far.shape[2]
+    is_end = jnp.logical_or(q == 0, q == line - 1)
+    is_next = jnp.logical_or(q == 1, q == line - 2)
+    inner = (jnp.where(q == 0, d + 2, d - 2), t)
+    outer = (jnp.where(q == 1, d - 2, d + 2), t)
 
     def local(src, dst, k):
         return pltpu.make_async_copy(src, dst, local_sem.at[k])
@@ -110,13 +122,25 @@
     for c in first:
         c.wait()
 
-    def line_copy(kind, way, s, slot):
+    def line_copy(kind, way, s, slot, short=False):
         ref = downs.at[slot] if kind == 0 else ups.at[slot]
+        if short:
+            ref = downs.at[slot, :, pl.ds(0, near)]
         send, recv = (zd_s, zd_r) if kind == 0 else (zu_s, zu_r)
         return remote(
             ref, ref, send.at[way, s], recv.at[way, s], above if way == 0 else below
         )
 
+    def to_end(way):
+        return q == line - 2 if way == 0 else q == 1
+
+    def both(kind, cond, short, act):
+        if kind == 1:
+            pl.when(cond)(lambda: act(False))
+        else:
+            pl.when(jnp.logical_and(cond, short))(lambda: act(True))
+            pl.when(jnp.logical_and(cond, jnp.logical_not(short)))(lambda: act(False))
+
     def sends(way, s):
         if way == 0:
             return jnp.logical_and(has_above, q - s >= 0)
@@ -132,9 +156,12 @@
         return q - 1 - s if way == 0 else q + 1 + s
 
     def send_line(kind, way, s):
-        @pl.when(sends(way, s))
-        def _():
-            line_copy(kind, way, s, sent_slot(way, s)).start()
+        both(
+            kind,
+            sends(way, s),
+            to_end(way),
+            lambda short: line_copy(kind, way, s, sent_slot(way, s), short).start(),
+        )
 
     def cross_copy(slot):
         return remote(picks.at[slot], ups_x.at[slot], xu_s.at[slot], xu_r.at[slot], across)
@@ -178,6 +205,25 @@
         c.start()
     x_rows.start()
     to1.start()
+    rest = pl.ds(near, width - near)
+    far_rows = [
+        remote(src, far.at[g], far_s.at[g], far_r.at[g], inner)
+        for g, src in enumerate((hid.at[t, :, rest], rows_x.at[:, rest]))
+    ]
+    far_places = [
+        remote(pos.at[g], far_pos.at[g], far_s.at[2 + g], far_r.at[2 + g], inner)
+        for g in (0, 1)
+    ]
+    far_back = [
+        remote(far_pack.at[g], far_got.at[g], far_s.at[4 + g], far_r.at[4 + g], outer)
+        for g in (0, 1)
+    ]
+
+    @pl.when(is_end)
+    def _():
+        far_places[0].start()
+        far_rows[0].start()
+
     send_line(1, 0, 0)
     send_line(1, 1, 0)
 
@@ -202,10 +248,11 @@
         m = jnp.where(wanted, 1, 0)
         return jnp.concatenate([m] * 4, axis=0) > 0
 
-    def shrink(which, slot, start=False):
-        source = hid[t] if which == 0 else rows_x[...]
+    def shrink(which, slot, start=False, short=False):
+        cols = pl.ds(0, near if short else width)
+        source = hid[t, :, cols] if which == 0 else rows_x[:, cols]
         value = lax.dot_general(
-            source, downs[slot], (((1,), (1,)), ((), ())), preferred_element_type=F32
+            source, downs[slot, :, cols], (((1,), (1,)), ((), ())), preferred_element_type=F32
         )
         value = jnp.where(
             keep(which, pos[which] == 2 * (2 * slot + p) + half), value, 0.0
@@ -227,9 +274,12 @@
     def down_step(s):
         for way in (0, 1):
 
-            @pl.when(arrives(way, s))
-            def _():
-                line_copy(0, way, s, arrived_slot(way, s)).wait_recv()
+            both(
+                0,
+                arrives(way, s),
+                is_end,
+                lambda short: line_copy(0, way, s, arrived_slot(way, s), short).wait_recv(),
+            )
 
             if s + 1 < line:
                 send_line(0, way, s + 1)
@@ -237,9 +287,12 @@
     def down_use(which, s):
         for way in (0, 1):
 
-            @pl.when(arrives(way, s))
-            def _():
-                shrink(which, arrived_slot(way, s))
+            both(
+                0,
+                arrives(way, s),
+                is_end,
+                lambda short: shrink(which, arrived_slot(way, s), False, short),
+            )
 
     def up_step(s):
         for way in (0, 1):
@@ -252,6 +305,41 @@
 
             if s + 1 < line:
                 send_line(1, way, s + 1)
+
+    rank = ADAPTER_RANK
+    fold = count // 2
+    left = lax.broadcasted_iota(jnp.int32, (fold, 2 * rank), 1) < rank
+
+    def pack(value):
+        both = value + pltpu.roll(value, rank, 1)
+        return jnp.where(left, both[:fold], both[fold:])
+
+    def unpack(value):
+        turned = pltpu.roll(value, rank, 1)
+        return jnp.concatenate(
+            [jnp.where(left, value, turned), jnp.where(left, turned, value)], axis=0
+        )
+
+    def far_use():
+        for g in (0, 1):
+            far_places[g].wait_recv()
+            far_rows[g].wait_recv()
+            far_part[...] = jnp.zeros_like(far_part)
+
+            @pl.loop(0, line - 1)
+            def _(i):
+                slot = i + jnp.where(q == 1, 1, 0)
+                value = lax.dot_general(
+                    far[g],
+                    downs[slot, :, rest],
+                    (((1,), (1,)), ((), ())),
+                    preferred_element_type=F32,
+                )
+                wanted = far_pos[g] == 2 * (2 * slot + p) + half
+                far_part[...] += jnp.where(keep(g, wanted), value, 0.0)
+
+            far_pack[g] = pack(far_part[...])
+            far_back[g].start()
 
     pass_on(0)
     pass_on(1)
@@ -263,6 +351,12 @@
     to1.wait_recv()
     base(t1, 1, False)
     x_rows.wait_recv()
+
+    @pl.when(is_end)
+    def _():
+        far_places[1].start()
+        far_rows[1].start()
+
     shrink(1, q, True)
     down_use(1, 0)
     base(t2, 2, False)
@@ -276,20 +370,14 @@
             base(t3, 3, False)
         if s < line - 2:
             up_step(s)
-
-    rank = ADAPTER_RANK
-    fold = count // 2
-    left = lax.broadcasted_iota(jnp.int32, (fold, 2 * rank), 1) < rank
-
-    def pack(value):
-        both = value + pltpu.roll(value, rank, 1)
-        return jnp.where(left, both[:fold], both[fold:])
-
-    def unpack(value):
-        turned = pltpu.roll(value, rank, 1)
-        return jnp.concatenate(
-            [jnp.where(left, value, turned), jnp.where(left, turned, value)], axis=0
-        )
+        if s == line - 3:
+            pl.when(is_next)(far_use)
+
+    @pl.when(is_end)
+    def _():
+        for g in (0, 1):
+            far_back[g].wait_recv()
+            part[g] += jnp.where(keep(g, pos[g] % 2 == half), unpack(far_got[g]), 0.0)
 
     packed[0] = pack(part[1])
     to_x = remote(packed.at[0], got.at[0], red_s.at[0], red_r.at[0], across)
@@ -341,14 +429,25 @@
         c.wait_send()
     for slot in range(line):
         cross_copy(slot).wait_send()
+    @pl.when(is_end)
+    def _():
+        for c in far_places + far_rows:
+            c.wait_send()
+
+    @pl.when(is_next)
+    def _():
+        for c in far_back:
+            c.wait_send()
+
     for s in range(line):
         for way in (0, 1):
-
-            @pl.when(sends(way, s))
-            def _():
-                slot = sent_slot(way, s)
-                line_copy(0, way, s, slot).wait_send()
-                line_copy(1, way, s, slot).wait_send()
+            for kind in (0, 1):
+                both(
+                    kind,
+                    sends(way, s),
+                    to_end(way),
+                    lambda short: line_copy(kind, way, s, sent_slot(way, s), short).wait_send(),
+                )
 
 
 def project(token_rows, weight, down, up, position, line):
@@ -393,6 +492,13 @@
             sems((line,)),
             sems((3,)),
             sems((3,)),
+            pltpu.VMEM((2, count, width * 3 // 8), BF16),
+            pltpu.VMEM((2, count // 4, pages), jnp.int32),
+            pltpu.VMEM((count, pages), F32),
+            pltpu.VMEM((2, count // 2, pages), F32),
+            pltpu.VMEM((2, count // 2, pages), F32),
+            sems((6,)),
+            sems((6,)),
         ],
         compiler_params=pltpu.CompilerParams(
             collective_id=0, has_side_effects=True, vmem_limit_bytes=56 * 2**20

time: 76.6 us -> 77.5 us (1.012)
  Pallas kernels: 70.6 us -> 71.5 us
    pallas_call x1, Pallas kernels: 65.9 us -> 66.8 us  [project(): pl.pallas_call(functools.partial(project_kernel, line), out_shape=jax.Sha...]
where the time goes in v3:
time: 77.5 us; the launch traced here: 77.3 us
  Pallas kernels  71.5 us (92%)
  local copies, waits for them, and re-layouts  4.87 us (6%)
  other arithmetic  0.91 us (1%)
    pallas_call x1, Pallas kernels, project(): pl.pallas_call(functools.partial(project_kernel, line), out_shape=jax.Sha...  66.8 us
    pallas_call x1, Pallas kernels, attend(): pl.pallas_call(functools.partial(attend_kernel, steps), grid=(requests //...  4.67 us
    unnamed x4, local copies, waits for them, and re-layouts  2.15 us

profile of v3, /device:TPU:0, one launch (start us, length us, event | category | flops | bytes accessed | tf_op | source)
XLA Modules:
  0.0 77.3 jit_solution(12502914146331144427)
XLA Ops:
  0.0 0.0 copy-start
  0.0 0.9 %select_reduce_fusion = s32[64]{0:T(128)S(1)} fusion(s32[16]{0:T(128)} %param.17, s32[64]{0:T(128)} %param.16), kind=kLoop, calls=%fused_computation.7 | loop fusion | flops 3008 | bytes 576 | tf_op jit(solution)/shard_map/reduce_sum | solution.py:563
  0.9 0.7 broadcast_in_dim.18.pos_hbm
  1.6 0.8 %broadcast_in_dim.30.len_ref = s32[64,1,128]{2,1,0:T(1,128)S(1)} broadcast(s32[64]{0:T(128)} %param.15), dimensions={0} | broadcast | bytes 33024 | tf_op jit(solution)/shard_map/broadcast_in_dim | solution.py:569
  2.4 1.0 %copy.21 = bf16[4,2,64,128]{3,0,2,1:T(4,128)(2,1)S(1)} copy(bf16[4,2,64,128]{3,2,1,0:T(8,128)(2,1)} %param.14) | data formatting | bytes 262144 | tf_op args[5]
  3.4 0.1 fusion.1
  3.5 66.8 %shard_map.91 = bf16[256,1024]{1,0:T(8,128)(2,1)} custom-call(bf16[256,2048]{1,0:T(8,128)(2,1)} %bitcast.24, bf16[8192,1024]{1,0:T(8,128)(2,1)} %w_hbm.1, bf16[128,2048]{1,0:T(8,128)(2,1)} %down_hbm.1, bf16[128,1024]{1,0:T(8,128)(2,1)} %up_hbm.1, s32[64,128]{1,0:T(8,128)} %broadcast_in_dim.18.pos_hbm), custom_call_target="tpu_custom_call" | custom-call | tf_op jit(solution)/shard_map/pallas_call | solution.py:459
  70.3 1.1 %copy.16 = bf16[32,8,8,128]{3,2,1,0:T(8,128)(2,1)S(1)} copy(bf16[32,8,8,128]{3,1,2,0:T(8,128)(2,1)} %bitcast.22) | data formatting | bytes 1048576
  71.4 0.1 copy_bitcast_fusion.1.q_ref
  71.5 0.0 copy-done
  71.5 4.7 %shard_map.92 = bf16[64,32,128]{2,1,0:T(8,128)(2,1)S(1)} custom-call(bf16[64,32,128]{2,1,0:T(8,128)(2,1)S(1)} %copy_bitcast_fusion.1.q_ref, bf16[2,64,128,128]{3,2,1,0:T(8,128)(2,1)S(1)} %copy-done, bf16[2,64,128,128]{3,2,1,0:T(8,128)(2,1)S(1)} %copy-done, bf16[64,16,128]{2,1,0:T(8,128)(2,1)S(1)} %get-tuple-element.6.nk_ref, ...), custom_call_target="tpu_custom_call" | custom-call | tf_op jit(solution)/shard_map/pallas_call | solution.py:543
  76.2 0.1 reshape.21
  76.4 1.0 %copy.20 = bf16[64,4,1024]{2,0,1:T(8,128)(2,1)} copy(bf16[64,4,1024]{2,1,0:T(4,128)(2,1)S(1)} %reshape.21) | data formatting | bytes 1048576 | tf_op jit(solution)/shard_map/reshape | solution.py:573
Async XLA Ops:
  0.0 71.5 %copy-start = (bf16[2,64,128,128]{3,2,1,0:T(8,128)(2,1)S(1)}, bf16[2,64,128,128]{3,2,1,0:T(8,128)(2,1)}, u32[]{:S(2)}) copy-start(bf16[2,64,128,128]{3,2,1,0:T(8,128)(2,1)} %v_ref.1) | copy-start | bytes 12582916

commit v4 on v3

--- a/solution.py
+++ b/solution.py
@@ -219,13 +219,14 @@
         for g in (0, 1)
     ]
 
+    send_line(1, 0, 0)
+    send_line(1, 1, 0)
+
     @pl.when(is_end)
     def _():
         far_places[0].start()
         far_rows[0].start()
 
-    send_line(1, 0, 0)
-    send_line(1, 1, 0)
 
     tile = 256
 

time: 77.5 us -> 75.1 us (0.969)
  Pallas kernels: 71.5 us -> 69 us
    pallas_call x1, Pallas kernels: 66.8 us -> 64.3 us  [project(): pl.pallas_call(functools.partial(project_kernel, line), out_shape=jax.Sha...]
where the time goes in v4:
time: 75.1 us; the launch traced here: 74.8 us
  Pallas kernels  69 us (92%)
  local copies, waits for them, and re-layouts  4.87 us (6%)
  other arithmetic  0.91 us (1%)
    pallas_call x1, Pallas kernels, project(): pl.pallas_call(functools.partial(project_kernel, line), out_shape=jax.Sha...  64.3 us
    pallas_call x1, Pallas kernels, attend(): pl.pallas_call(functools.partial(attend_kernel, steps), grid=(requests //...  4.67 us
    unnamed x4, local copies, waits for them, and re-layouts  2.15 us

profile of v4, /device:TPU:0, one launch (start us, length us, event | category | flops | bytes accessed | tf_op | source)
XLA Modules:
  0.0 74.8 jit_solution(15708068995027681103)
XLA Ops:
  0.0 0.0 copy-start
  0.0 0.9 %select_reduce_fusion = s32[64]{0:T(128)S(1)} fusion(s32[16]{0:T(128)} %param.17, s32[64]{0:T(128)} %param.16), kind=kLoop, calls=%fused_computation.7 | loop fusion | flops 3008 | bytes 576 | tf_op jit(solution)/shard_map/reduce_sum | solution.py:564
  0.9 0.7 broadcast_in_dim.18.pos_hbm
  1.6 0.8 %broadcast_in_dim.30.len_ref = s32[64,1,128]{2,1,0:T(1,128)S(1)} broadcast(s32[64]{0:T(128)} %param.15), dimensions={0} | broadcast | bytes 33024 | tf_op jit(solution)/shard_map/broadcast_in_dim | solution.py:570
  2.4 1.0 %copy.21 = bf16[4,2,64,128]{3,0,2,1:T(4,128)(2,1)S(1)} copy(bf16[4,2,64,128]{3,2,1,0:T(8,128)(2,1)} %param.14) | data formatting | bytes 262144 | tf_op args[5]
  3.4 0.1 fusion.1
  3.5 64.3 %shard_map.91 = bf16[256,1024]{1,0:T(8,128)(2,1)} custom-call(bf16[256,2048]{1,0:T(8,128)(2,1)} %bitcast.24, bf16[8192,1024]{1,0:T(8,128)(2,1)} %w_hbm.1, bf16[128,2048]{1,0:T(8,128)(2,1)} %down_hbm.1, bf16[128,1024]{1,0:T(8,128)(2,1)} %up_hbm.1, s32[64,128]{1,0:T(8,128)} %broadcast_in_dim.18.pos_hbm), custom_call_target="tpu_custom_call" | custom-call | tf_op jit(solution)/shard_map/pallas_call | solution.py:460
  67.8 1.1 %copy.16 = bf16[32,8,8,128]{3,2,1,0:T(8,128)(2,1)S(1)} copy(bf16[32,8,8,128]{3,1,2,0:T(8,128)(2,1)} %bitcast.22) | data formatting | bytes 1048576
  68.9 0.1 copy_bitcast_fusion.1.q_ref
  69.0 0.0 copy-done
  69.1 4.7 %shard_map.92 = bf16[64,32,128]{2,1,0:T(8,128)(2,1)S(1)} custom-call(bf16[64,32,128]{2,1,0:T(8,128)(2,1)S(1)} %copy_bitcast_fusion.1.q_ref, bf16[2,64,128,128]{3,2,1,0:T(8,128)(2,1)S(1)} %copy-done, bf16[2,64,128,128]{3,2,1,0:T(8,128)(2,1)S(1)} %copy-done, bf16[64,16,128]{2,1,0:T(8,128)(2,1)S(1)} %get-tuple-element.6.nk_ref, ...), custom_call_target="tpu_custom_call" | custom-call | tf_op jit(solution)/shard_map/pallas_call | solution.py:544
  73.7 0.1 reshape.21
  73.9 1.0 %copy.20 = bf16[64,4,1024]{2,0,1:T(8,128)(2,1)} copy(bf16[64,4,1024]{2,1,0:T(4,128)(2,1)S(1)} %reshape.21) | data formatting | bytes 1048576 | tf_op jit(solution)/shard_map/reshape | solution.py:574
Async XLA Ops:
  0.0 69.0 %copy-start = (bf16[2,64,128,128]{3,2,1,0:T(8,128)(2,1)S(1)}, bf16[2,64,128,128]{3,2,1,0:T(8,128)(2,1)}, u32[]{:S(2)}) copy-start(bf16[2,64,128,128]{3,2,1,0:T(8,128)(2,1)} %v_ref.1) | copy-start | bytes 12582916
